TPU v7x, 128 devices: a whole 4x4x4 slice. The times are simulated.
128 devices in a mesh: frames: 64 (over z, y, x_lo, core), dp: 2 (over x_hi).
Axes of the slice: x: 4 (x_hi: 2, x_lo: 2; x = x_hi * 2 + x_lo), y: 4, z: 4, core: 2. Of those that a mesh axis runs over, the one named last changes fastest.
Arguments:
- shifted: bfloat16 [2, 256, 16, 16, 640], P('dp', 'frames'), may hold values from -6 to 6
- out_grad: bfloat16 [2, 256, 16, 16, 640], P('dp', 'frames'), may hold values from -6 to 6
- conv_weight: bfloat16 [640, 5760], P('frames'), may hold values from -0.078125 to 0.078125
- norm_gain: float32 [640], replicated, may hold values from 0.5 to 2
- norm_bias: float32 [640], replicated, may hold values from -4 to 4
- shift_fwd: int32 [80], replicated, may hold values from 0 to 639, as said below
- shift_bwd: int32 [80], replicated, may hold values from 0 to 639, as said below
Outputs:
- in_grad: bfloat16 [2, 256, 16, 16, 640], P('dp', 'frames')
- weight_grad: float32 [640, 5760], P('frames')
- gain_grad: float32 [640], replicated
- bias_grad: float32 [640], replicated
Inputs may be any that keep to these rules, and one draw needn't show every extreme that they name: `shift_fwd`: 80 distinct channel numbers, none of them in shift_bwd. `shift_bwd`: 80 distinct channel numbers, none of them in shift_fwd.
All inputs are finite; a program needn't handle non-finite values.
Results may differ from a plain program's by a relative error of at most 0.003.
Values may be sent and summed in bfloat16 or wider, within the bound.
A program may use at most 128 MiB of HBM per device.

v0:
```python
import jax
import jax.numpy as jnp
from jax import lax
from jax.sharding import PartitionSpec as P

GROUP_CH = 20
epsilon = 1e-05


def with_halo(x, sides, width):
    for axis, dim in sides:
        size, length = (lax.axis_size(axis), x.shape[dim])
        up = [(i, (i + 1) % size) for i in range(size - 1)]
        down = [(j, i) for i, j in up]
        last = lax.slice_in_dim(x, length - width, length, axis=dim)
        first = lax.slice_in_dim(x, 0, width, axis=dim)
        before = lax.ppermute(last, axis, up)
        after = lax.ppermute(first, axis, down)
        x = jnp.concatenate([before, x, after], axis=dim)
    return x


def pad_space(values):
    return jnp.pad(values, ((0, 0), (1, 1), (1, 1), (0, 0)))


def on_device(shifted, out_grad, conv_weight, norm_gain, norm_bias, shift_fwd, shift_bwd):
    frames_local = shifted[0]
    grad_local = out_grad[0]
    frame_count, row_count, col_count, channels = frames_local.shape
    groups = channels // GROUP_CH
    whole_weight = lax.all_gather(conv_weight, "frames", axis=0, tiled=True)
    values = frames_local.astype(jnp.float32).reshape(
        frame_count, row_count * col_count, groups, GROUP_CH
    )
    center = jnp.mean(values, axis=(1, 3), keepdims=True)
    spread = jnp.mean(jnp.square(values - center), axis=(1, 3), keepdims=True)
    inverse = lax.rsqrt(spread + epsilon)
    grouped_normed = (values - center) * inverse
    normed = grouped_normed.reshape(frame_count, row_count, col_count, channels)
    before = normed * norm_gain + norm_bias
    activation = jax.nn.silu(before).astype(jnp.bfloat16)
    act_padded = pad_space(activation)
    grad_padded = pad_space(grad_local)
    grad_rows = grad_local.reshape(-1, channels)
    act_grad = jnp.zeros((grad_rows.shape[0], channels), jnp.float32)
    for tap_index in range(9):
        row_off, col_off = divmod(tap_index, 3)
        grad_view = grad_padded[
            :, 2 - row_off : 2 - row_off + row_count, 2 - col_off : 2 - col_off + col_count, :
        ].reshape(-1, channels)
        act_grad = act_grad + jnp.dot(
            grad_view,
            whole_weight[:, tap_index * channels : (tap_index + 1) * channels],
            preferred_element_type=jnp.float32,
        )
    scale = float(
        lax.axis_size("dp") * lax.axis_size("frames") * frame_count * row_count * col_count
    ) ** (-0.5)
    parts = []
    for tap_index in range(9):
        row_off, col_off = divmod(tap_index, 3)
        act_view = act_padded[
            :, row_off : row_off + row_count, col_off : col_off + col_count, :
        ].reshape(-1, channels)
        parts.append(
            lax.dot_general(
                grad_rows, act_view, (((0,), (0,)), ((), ())), preferred_element_type=jnp.float32
            )
        )
    kernel_shard = lax.psum_scatter(
        jnp.concatenate(parts, axis=1), "frames", scatter_dimension=0, tiled=True
    )
    kernel_shard = lax.psum(kernel_shard, "dp")
    weight_grad = kernel_shard * scale
    sigmoid_val = jax.nn.sigmoid(before)
    pre_grad = act_grad.reshape(before.shape) * sigmoid_val * (1.0 + before * (1.0 - sigmoid_val))
    gain_part = jnp.sum(pre_grad * normed, axis=(0, 1, 2))
    bias_part = jnp.sum(pre_grad, axis=(0, 1, 2))
    gain_total, bias_total = lax.psum((gain_part, bias_part), ("frames", "dp"))
    norm_grad = (pre_grad * norm_gain).reshape(values.shape)
    first_mean = jnp.mean(norm_grad, axis=(1, 3), keepdims=True)
    second_mean = jnp.mean(norm_grad * grouped_normed, axis=(1, 3), keepdims=True)
    shifted_grad = (
        ((norm_grad - first_mean - grouped_normed * second_mean) * inverse)
        .reshape(frames_local.shape)
        .astype(jnp.bfloat16)
    )
    channel_ids = jnp.arange(channels, dtype=jnp.int32)
    forward_match = channel_ids[None, :] == shift_fwd[:, None]
    backward_match = channel_ids[None, :] == shift_bwd[:, None]
    forward_select = forward_match.astype(jnp.bfloat16)
    backward_select = backward_match.astype(jnp.bfloat16)
    forward_mask = jnp.any(forward_match, axis=0)
    backward_mask = jnp.any(backward_match, axis=0)
    plane = row_count * col_count
    first_frame = shifted_grad[0].reshape(plane, channels)
    last_frame = shifted_grad[frame_count - 1].reshape(plane, channels)
    contract_channels = (((1,), (1,)), ((), ()))
    rim_first = lax.dot_general(
        forward_select, first_frame, contract_channels, preferred_element_type=jnp.float32
    ).astype(jnp.bfloat16)
    rim_last = lax.dot_general(
        backward_select, last_frame, contract_channels, preferred_element_type=jnp.float32
    ).astype(jnp.bfloat16)
    extended = with_halo(jnp.stack([rim_first, rim_last]), (("frames", 0),), 1)
    contract_fold = (((0,), (0,)), ((), ()))
    from_prev = lax.dot_general(
        extended[0], backward_select, contract_fold, preferred_element_type=jnp.float32
    ).astype(jnp.bfloat16)
    from_next = lax.dot_general(
        extended[3], forward_select, contract_fold, preferred_element_type=jnp.float32
    ).astype(jnp.bfloat16)
    from_prev = from_prev.reshape(1, row_count, col_count, channels)
    from_next = from_next.reshape(1, row_count, col_count, channels)
    later = jnp.concatenate([shifted_grad[1:], from_next], axis=0)
    earlier = jnp.concatenate([from_prev, shifted_grad[:-1]], axis=0)
    in_grad = jnp.where(forward_mask, later, jnp.where(backward_mask, earlier, shifted_grad))
    return (in_grad[None], weight_grad, gain_total * scale, bias_total * scale)


def solution(mesh):
    in_specs = (
        P("dp", "frames", None, None, None),
        P("dp", "frames", None, None, None),
        P("frames", None),
        P(),
        P(),
        P(),
        P(),
    )
    out_specs = (P("dp", "frames", None, None, None), P("frames", None), P(), P())
    return jax.shard_map(
        on_device, mesh=mesh, in_specs=in_specs, out_specs=out_specs, check_vma=False
    )
```

profile of v0, /device:TPU:1, one launch (start us, length us, event | category | flops | bytes accessed | tf_op | source)
XLA Modules:
  0.0 923.6 jit_solution(15676079137542957894)
XLA Ops:
  7.2 0.7 all-gather.3.cloned.1.call-update
  8.0 21.9 %reshape.226 = f32[4,256,32,20]{3,2,1,0:T(8,128)} reshape(bf16[1,4,16,16,640]{4,3,2,1,0:T(8,128)(2,1)} %param.7) | data formatting | bytes 3932160 | tf_op jit(solution)/shard_map/convert_element_type | solution.py:33
  29.9 0.2 convert_reduce_fusion
  30.1 0.1 reduce_sum.69
  30.2 0.1 reduce_sum.70
  30.5 0.1 sub.85
  30.6 0.4 multiply_reduce_fusion.2
  31.0 0.1 reduce_sum.72
  31.1 0.1 reduce_sum.73
  31.2 0.1 copy.34
  31.4 0.1 mul.190
  31.5 11.5 %copy.33 = f32[4,256,32,20]{1,0,3,2:T(4,128)} copy(f32[4,256,32,20]{3,2,1,0:T(8,128)} %reshape.226) | data formatting | bytes 5242880 | tf_op jit(solution)/shard_map/convert_element_type | solution.py:33
  43.0 0.1 add.134
  43.1 0.1 mul.201
  43.2 8.8 pad_slice_fusion.8
  52.0 78.7 %all-gather.3.cloned.1.call-done = bf16[64,10,5760]{2,1,0:T(8,128)(2,1)} async-done(((bf16[1,10,5760]{2,1,0:T(8,128)(2,1)}), bf16[64,10,5760]{2,1,0:T(8,128)(2,1)}) %all-gather.3.cloned.1.call-update) | async-done | bytes 7372816 | tf_op jit(solution)/shard_map/all_gather | solution.py:32
  130.7 13.8 %reshape.229 = bf16[640,5760]{1,0:T(8,128)(2,1)} reshape(bf16[64,10,5760]{2,1,0:T(8,128)(2,1)} %all-gather.3.cloned.1.call-done) | data formatting | bytes 14745600
  144.6 3.0 fusion.4
  147.6 0.7 copy-done.1
  148.3 0.3 copy-done.11
  148.6 1.3 fusion.6
  149.9 1.3 fusion.8
  151.3 1.3 fusion.10
  152.6 1.3 fusion.12
  154.0 1.3 fusion.14
  155.3 2.8 fusion.18
  158.1 2.8 fusion.16
  160.9 6.2 fusion.28
  167.1 3.3 copy.31
  170.3 4.2 reshape.215
  174.5 16.5 %fusion.29 = (f32[4,32]{0,1:T(8,128)S(1)}, f32[4,32]{0,1:T(8,128)S(1)}) fusion(f32[4,32]{0,1:T(8,128)S(1)} %copy.34, f32[4,256,32,20]{1,0,3,2:T(4,128)} %copy.33, f32[4,32]{0,1:T(8,128)S(1)} %copy.32, f32[4,256,32,20]{1,0,3,2:T(4,128)} %reshape.215, f32[32,20]{1,0:T(8,128)S(1)} %add.134, f32[32,20]{1,0:T(8,128)S(1)} %mul.201), kind=kLoop, calls=%fused_computation.88 | loop fusion | flops 10485504 | bytes 5250048 | tf_op jit(solution)/shard_map/reduce_sum | solution.py:82
  191.2 0.1 mul.210
  191.5 0.1 sub.95
  191.6 3.6 multiply_convert_fusion
  195.2 3.0 pad_slice_fusion
  198.2 2.4 bitcast_dynamic-update-slice_fusion.8
  200.6 2.4 bitcast_dynamic-update-slice_fusion.7
  203.0 2.4 bitcast_dynamic-update-slice_fusion.6
  205.5 2.4 bitcast_dynamic-update-slice_fusion.5
  207.9 2.4 bitcast_dynamic-update-slice_fusion.4
  210.3 2.4 bitcast_dynamic-update-slice_fusion.3
  212.7 2.5 bitcast_dynamic-update-slice_fusion.2
  215.2 2.4 bitcast_dynamic-update-slice_fusion.1
  217.6 2.4 bitcast_dynamic-update-slice_fusion
  220.1 0.6 copy-done.16
  220.7 0.6 dynamic-slice
  222.0 0.1 fusion.20
  222.2 0.2 fusion.1
  222.4 2.2 collective-permute-start
  224.6 0.2 fusion.2
  224.9 3.4 collective-permute-start.1
  228.2 67.9 %all-reduce.3 = (f32[640]{0:T(1024)S(1)}, f32[640]{0:T(1024)S(1)}) all-reduce(f32[640]{0:T(1024)S(1)} %get-tuple-element.25, f32[640]{0:T(1024)S(1)} %get-tuple-element.24), channel_id=1, replica_groups=mesh['frames'=64,'dp'=2] {'frames','dp'}, use_global_device_ids=true, to_apply=%region_11.12 | all-reduce | flops 1280 | bytes 10240 | tf_op jit(solution)/shard_map/psum | solution.py:80
  296.1 1.5 slice_bitcast_fusion
  297.6 0.6 broadcast_multiply_fusion.1
  298.2 1.0 convolution_convert_fusion.1
  299.2 1.0 convolution_convert_fusion
  300.3 516.5 %all-reduce.9.cloned.1.call-done = f32[640,5760]{0,1:T(8,128)} async-done(((f32[640,5760]{0,1:T(8,128)}), f32[640,5760]{0,1:T(8,128)}) %all-reduce.9.cloned.1.call-update) | async-done | bytes 14745616
  816.7 5.1 constant_dynamic-slice_fusion
  821.8 1.2 copy-done.2
  823.0 0.3 copy-done.3
  823.3 4.4 maximum_select_fusion
  827.7 82.4 %all-reduce.7.cloned.1.call-done = f32[10,5760]{0,1:T(8,128)} async-done(((f32[10,5760]{0,1:T(8,128)}), f32[10,5760]{0,1:T(8,128)}) %all-reduce.7.cloned.1.call-update) | async-done | bytes 230416 | tf_op jit(solution)/shard_map/psum | solution.py:74
  910.1 3.7 broadcast_multiply_fusion
  913.8 3.0 copy.37
  (48 shorter events, 0.8 us)
Async XLA Ops:
  7.2 123.5 %all-gather.3.cloned.1.call-start = ((), (), s32[]{:S(2)}) async-start(), calls=%async_computation.1 | async-start | bytes 11980800 | tf_op jit(solution)/shard_map/all_gather | solution.py:32
  7.9 22.0 %copy-start = (bf16[1,4,16,16,640]{4,3,2,1,0:T(8,128)(2,1)S(1)}, bf16[1,4,16,16,640]{4,3,2,1,0:T(8,128)(2,1)}, u32[]{:S(2)}) copy-start(bf16[1,4,16,16,640]{4,3,2,1,0:T(8,128)(2,1)} %param.7) | copy-start | bytes 3932164
  7.9 808.8 %all-reduce.9.cloned.1.call-start = ((), (), s32[]{:S(2)}) async-start(), calls=%async_computation.2 | async-start | bytes 29491200
  31.5 11.5 %copy-start.12 = (f32[640]{0:T(1024)S(1)}, f32[640]{0:T(1024)}, u32[]{:S(2)}) copy-start(f32[640]{0:T(1024)} %param.11) | copy-start | bytes 7684
  31.5 11.6 %copy-start.13 = (f32[640]{0:T(1024)S(1)}, f32[640]{0:T(1024)}, u32[]{:S(2)}) copy-start(f32[640]{0:T(1024)} %param.10) | copy-start | bytes 7684
  144.5 3.7 copy-start.1
  144.6 4.0 copy-start.11
  148.6 1.3 copy-start.10
  149.9 1.3 copy-start.4
  151.3 1.3 copy-start.9
  152.6 1.3 copy-start.8
  154.0 1.3 copy-start.7
  155.3 2.8 copy-start.6
  195.2 3.0 copy-start.5
  220.1 0.7 copy-start.16
  220.1 1.9 copy-start.14
  220.1 1.9 copy-start.15
  220.1 690.0 %all-reduce.7.cloned.1.call-start = ((), (), s32[]{:S(2)}) async-start(), calls=%async_computation | async-start | bytes 5898240 | tf_op jit(solution)/shard_map/psum | solution.py:74
  222.4 75.8 %collective-permute-start = (bf16[1,80,256]{2,1,0:T(8,128)(2,1)S(1)}, bf16[1,80,256]{2,1,0:T(8,128)(2,1)S(1)}, u32[]{:S(2)}, u32[]{:S(2)}) collective-permute-start(bf16[1,80,256]{2,1,0:T(8,128)(2,1)S(1)} %fusion.1), channel_id=1, source_target_pairs={{2,0},{4,2},{6,4},{8,6},{10,8},{12,10},{14,12},{16,14},{18,16},{20... | collective-permute-start | bytes 122888 | tf_op jit(solution)/shard_map/ppermute | solution.py:18
  224.9 74.4 %collective-permute-start.1 = (bf16[1,80,256]{2,1,0:T(8,128)(2,1)S(1)}, bf16[1,80,256]{2,1,0:T(8,128)(2,1)S(1)}, u32[]{:S(2)}, u32[]{:S(2)}) collective-permute-start(bf16[1,80,256]{2,1,0:T(8,128)(2,1)S(1)} %fusion.2), channel_id=1, source_target_pairs={{0,2},{2,4},{4,6},{6,8},{8,10},{10,12},{12,14},{14,16},{16,18},{18... | collective-permute-start | bytes 122888 | tf_op jit(solution)/shard_map/ppermute | solution.py:17
  821.8 1.2 copy-start.2
  821.8 1.5 copy-start.3
Sparse Core Ops, SparseCore 0:
  9.7 120.9 all-gather.2
  220.2 596.4 all-reduce.8
  822.0 88.0 all-reduce.6
where the time goes:
time: 929 us; the launch traced here: 924 us
  waiting for transfers between devices  678 us (73%)
  local copies, waits for them, and re-layouts  81.4 us (9%)
  blocking collectives  67.9 us (7%)
  matrix products  45.7 us (5%)
  other arithmetic  29.7 us (3%)
  between operations  15 us (2%)
    unnamed x4, waiting for transfers between devices  517 us
    psum x1, waiting for transfers between devices, on_device(): kernel_shard = lax.psum(kernel_shard, 'dp')  82.4 us
    all_gather x1, waiting for transfers between devices, on_device(): whole_weight = lax.all_gather(conv_weight, 'frames', axis=0, tiled=True)  78.7 us
    psum x1, blocking collectives, on_device(): gain_total, bias_total = lax.psum((gain_part, bias_part), ('frames', 'dp'))  67.9 us
    convert_element_type x2, local copies, waits for them, and re-layouts, on_device(): frames_local.astype(jnp.float32)  33.4 us
    unnamed x38, local copies, waits for them, and re-layouts  25.6 us
    dot_general x9, matrix products, on_device(): lax.dot_general(grad_rows, act_view, (((0,), (0,)), ((), ())), preferred_...  21.8 us
    dot_general x9, matrix products, on_device(): jnp.dot(grad_view, whole_weight[:, tap_index * channels:(tap_index + 1) *...  21.3 us
  transfers between devices with their start and end apart: 5, of which 3 were waited for; matrix products, arithmetic and copies ran while one was open for 6% of the time, Pallas kernels for 0%

commit v1 on v0

--- a/solution.py
+++ b/solution.py
@@ -77,7 +77,7 @@
     pre_grad = act_grad.reshape(before.shape) * sigmoid_val * (1.0 + before * (1.0 - sigmoid_val))
     gain_part = jnp.sum(pre_grad * normed, axis=(0, 1, 2))
     bias_part = jnp.sum(pre_grad, axis=(0, 1, 2))
-    gain_total, bias_total = lax.psum((gain_part, bias_part), ("frames", "dp"))
+    gain_total, bias_total = lax.psum(lax.psum((gain_part, bias_part), "dp"), "frames")
     norm_grad = (pre_grad * norm_gain).reshape(values.shape)
     first_mean = jnp.mean(norm_grad, axis=(1, 3), keepdims=True)
     second_mean = jnp.mean(norm_grad * grouped_normed, axis=(1, 3), keepdims=True)

time: 929 us -> 915 us (0.985)
  blocking collectives: 67.9 us -> 146 us
  waiting for transfers between devices: 678 us -> 602 us
  other arithmetic: 29.7 us -> 18.9 us
    psum x1 -> x2, blocking collectives: 67.9 us -> 146 us  [the longest x1 140 us: on_device(): lax.psum(lax.psum((gain_part, bias_part), 'dp'), 'frames')]
    unnamed x4, waiting for transfers between devices: 517 us -> 441 us
    reduce_sum x1, other arithmetic: 16.5 us -> 5.68 us  [on_device(): first_mean = jnp.mean(norm_grad, axis=(1, 3), keepdims=True)]
where the time goes in v1:
time: 915 us; the launch traced here: 914 us
  waiting for transfers between devices  602 us (66%)
  blocking collectives  146 us (16%)
  local copies, waits for them, and re-layouts  81 us (9%)
  matrix products  45.7 us (5%)
  other arithmetic  18.9 us (2%)
  between operations  14.7 us (2%)
    unnamed x4, waiting for transfers between devices  441 us
    psum x1, blocking collectives, on_device(): lax.psum(lax.psum((gain_part, bias_part), 'dp'), 'frames')  140 us
    psum x1, waiting for transfers between devices, on_device(): kernel_shard = lax.psum(kernel_shard, 'dp')  82.4 us
    all_gather x1, waiting for transfers between devices, on_device(): whole_weight = lax.all_gather(conv_weight, 'frames', axis=0, tiled=True)  78.7 us
    convert_element_type x2, local copies, waits for them, and re-layouts, on_device(): frames_local.astype(jnp.float32)  33.4 us
    unnamed x38, local copies, waits for them, and re-layouts  25.3 us
    dot_general x9, matrix products, on_device(): lax.dot_general(grad_rows, act_view, (((0,), (0,)), ((), ())), preferred_...  21.8 us
    dot_general x9, matrix products, on_device(): jnp.dot(grad_view, whole_weight[:, tap_index * channels:(tap_index + 1) *...  21.3 us
  transfers between devices with their start and end apart: 5, of which 3 were waited for; matrix products, arithmetic and copies ran while one was open for 6% of the time, Pallas kernels for 0%

profile of v1, /device:TPU:1, one launch (start us, length us, event | category | flops | bytes accessed | tf_op | source)
XLA Modules:
  0.0 914.2 jit_solution(15801352893657435228)
XLA Ops:
  7.2 0.7 all-gather.3.cloned.1.call-update
  8.0 21.9 %reshape.226 = f32[4,256,32,20]{3,2,1,0:T(8,128)} reshape(bf16[1,4,16,16,640]{4,3,2,1,0:T(8,128)(2,1)} %param.7) | data formatting | bytes 3932160 | tf_op jit(solution)/shard_map/convert_element_type | solution.py:33
  29.9 0.2 convert_reduce_fusion
  30.1 0.1 reduce_sum.69
  30.2 0.1 reduce_sum.70
  30.5 0.1 sub.85
  30.6 0.4 multiply_reduce_fusion.2
  31.0 0.1 reduce_sum.72
  31.1 0.1 reduce_sum.73
  31.4 0.1 mul.190
  31.5 11.5 %copy.33 = f32[4,256,32,20]{1,0,3,2:T(4,128)} copy(f32[4,256,32,20]{3,2,1,0:T(8,128)} %reshape.226) | data formatting | bytes 5242880 | tf_op jit(solution)/shard_map/convert_element_type | solution.py:33
  43.0 0.1 add.138
  43.1 0.1 mul.201
  43.2 8.8 pad_slice_fusion.8
  52.0 78.7 %all-gather.3.cloned.1.call-done = bf16[64,10,5760]{2,1,0:T(8,128)(2,1)} async-done(((bf16[1,10,5760]{2,1,0:T(8,128)(2,1)}), bf16[64,10,5760]{2,1,0:T(8,128)(2,1)}) %all-gather.3.cloned.1.call-update) | async-done | bytes 7372816 | tf_op jit(solution)/shard_map/all_gather | solution.py:32
  130.7 13.5 %reshape.229 = bf16[640,5760]{1,0:T(8,128)(2,1)} reshape(bf16[64,10,5760]{2,1,0:T(8,128)(2,1)} %all-gather.3.cloned.1.call-done) | data formatting | bytes 14745600
  144.2 3.0 fusion.4
  147.2 0.7 copy-done.1
  147.9 0.3 copy-done.11
  148.2 1.3 fusion.6
  149.6 1.3 fusion.8
  150.9 1.3 fusion.10
  152.3 1.3 fusion.12
  153.6 1.3 fusion.14
  155.0 2.8 fusion.18
  157.7 2.8 fusion.16
  160.6 6.2 fusion.28
  166.7 3.3 copy.31
  170.0 4.2 reshape.215
  174.2 5.7 fusion.29
  180.0 0.1 mul.210
  180.3 0.1 sub.95
  180.4 3.6 multiply_convert_fusion
  184.0 3.0 pad_slice_fusion
  187.0 2.4 bitcast_dynamic-update-slice_fusion.8
  189.4 2.4 bitcast_dynamic-update-slice_fusion.7
  191.9 2.4 bitcast_dynamic-update-slice_fusion.6
  194.3 2.4 bitcast_dynamic-update-slice_fusion.5
  196.7 2.4 bitcast_dynamic-update-slice_fusion.4
  199.1 2.4 bitcast_dynamic-update-slice_fusion.3
  201.5 2.5 bitcast_dynamic-update-slice_fusion.2
  204.0 2.4 bitcast_dynamic-update-slice_fusion.1
  206.5 2.4 bitcast_dynamic-update-slice_fusion
  209.0 0.6 copy-done.16
  209.5 0.6 dynamic-slice
  210.8 0.1 fusion.20
  211.0 0.2 fusion.1
  211.2 2.2 collective-permute-start
  213.4 0.2 fusion.2
  213.7 3.4 collective-permute-start.1
  217.1 5.9 all-reduce.4
  223.0 140.5 %all-reduce.3 = (f32[640]{0:T(1024)S(1)}, f32[640]{0:T(1024)S(1)}) all-reduce(f32[640]{0:T(1024)S(1)} %get-tuple-element.30, f32[640]{0:T(1024)S(1)} %get-tuple-element.31), channel_id=1, replica_groups=mesh['frames'=64,'dp'=2] {'frames'}, use_global_device_ids=true, to_apply=%region_12.13 | all-reduce | flops 1280 | bytes 10240 | tf_op jit(solution)/shard_map/psum | solution.py:80
  363.5 1.5 slice_bitcast_fusion
  365.0 0.6 broadcast_multiply_fusion.1
  365.6 1.0 convolution_convert_fusion.1
  366.6 1.0 convolution_convert_fusion
  367.6 439.9 %all-reduce.10.cloned.1.call-done = f32[640,5760]{0,1:T(8,128)} async-done(((f32[640,5760]{0,1:T(8,128)}), f32[640,5760]{0,1:T(8,128)}) %all-reduce.10.cloned.1.call-update) | async-done | bytes 14745616
  807.6 5.1 constant_dynamic-slice_fusion
  812.7 1.2 copy-done.2
  813.8 0.3 copy-done.3
  814.1 4.4 maximum_select_fusion
  818.5 82.4 %all-reduce.8.cloned.1.call-done = f32[10,5760]{0,1:T(8,128)} async-done(((f32[10,5760]{0,1:T(8,128)}), f32[10,5760]{0,1:T(8,128)}) %all-reduce.8.cloned.1.call-update) | async-done | bytes 230416 | tf_op jit(solution)/shard_map/psum | solution.py:74
  900.9 3.7 broadcast_multiply_fusion
  904.6 3.0 copy.37
  (49 shorter events, 0.9 us)
Async XLA Ops:
  7.2 123.5 %all-gather.3.cloned.1.call-start = ((), (), s32[]{:S(2)}) async-start(), calls=%async_computation.1 | async-start | bytes 11980800 | tf_op jit(solution)/shard_map/all_gather | solution.py:32
  7.9 22.0 %copy-start = (bf16[1,4,16,16,640]{4,3,2,1,0:T(8,128)(2,1)S(1)}, bf16[1,4,16,16,640]{4,3,2,1,0:T(8,128)(2,1)}, u32[]{:S(2)}) copy-start(bf16[1,4,16,16,640]{4,3,2,1,0:T(8,128)(2,1)} %param.7) | copy-start | bytes 3932164
  7.9 799.7 %all-reduce.10.cloned.1.call-start = ((), (), s32[]{:S(2)}) async-start(), calls=%async_computation.2 | async-start | bytes 29491200
  31.5 11.5 %copy-start.12 = (f32[640]{0:T(1024)S(1)}, f32[640]{0:T(1024)}, u32[]{:S(2)}) copy-start(f32[640]{0:T(1024)} %param.11) | copy-start | bytes 7684
  31.5 11.6 %copy-start.13 = (f32[640]{0:T(1024)S(1)}, f32[640]{0:T(1024)}, u32[]{:S(2)}) copy-start(f32[640]{0:T(1024)} %param.10) | copy-start | bytes 7684
  144.2 3.7 copy-start.1
  144.2 4.1 copy-start.11
  148.2 1.3 copy-start.10
  149.6 1.3 copy-start.4
  150.9 1.3 copy-start.9
  152.3 1.3 copy-start.8
  153.6 1.3 copy-start.7
  154.9 2.8 copy-start.6
  184.0 3.0 copy-start.5
  208.9 0.7 copy-start.16
  208.9 1.9 copy-start.14
  208.9 1.9 copy-start.15
  208.9 692.0 %all-reduce.8.cloned.1.call-start = ((), (), s32[]{:S(2)}) async-start(), calls=%async_computation | async-start | bytes 5898240 | tf_op jit(solution)/shard_map/psum | solution.py:74
  211.2 154.3 %collective-permute-start = (bf16[1,80,256]{2,1,0:T(8,128)(2,1)S(1)}, bf16[1,80,256]{2,1,0:T(8,128)(2,1)S(1)}, u32[]{:S(2)}, u32[]{:S(2)}) collective-permute-start(bf16[1,80,256]{2,1,0:T(8,128)(2,1)S(1)} %fusion.1), channel_id=1, source_target_pairs={{2,0},{4,2},{6,4},{8,6},{10,8},{12,10},{14,12},{16,14},{18,16},{20... | collective-permute-start | bytes 122888 | tf_op jit(solution)/shard_map/ppermute | solution.py:18
  213.7 152.9 %collective-permute-start.1 = (bf16[1,80,256]{2,1,0:T(8,128)(2,1)S(1)}, bf16[1,80,256]{2,1,0:T(8,128)(2,1)S(1)}, u32[]{:S(2)}, u32[]{:S(2)}) collective-permute-start(bf16[1,80,256]{2,1,0:T(8,128)(2,1)S(1)} %fusion.2), channel_id=1, source_target_pairs={{0,2},{2,4},{4,6},{6,8},{8,10},{10,12},{12,14},{14,16},{16,18},{18... | collective-permute-start | bytes 122888 | tf_op jit(solution)/shard_map/ppermute | solution.py:17
  812.6 1.2 copy-start.2
  812.6 1.5 copy-start.3
Sparse Core Ops, SparseCore 0:
  9.7 120.9 all-gather.2
  209.0 598.4 all-reduce.9
  812.8 88.0 all-reduce.7
